TPU v7x, 256 devices: a whole 4x4x8 slice. The times are simulated.
256 devices in a mesh: row: 128 (over z, y_lo, x, core), col: 2 (over y_hi).
Axes of the slice: x: 4, y: 4 (y_hi: 2, y_lo: 2; y = y_hi * 2 + y_lo), z: 8, core: 2. Of those that a mesh axis runs over, the one named last changes fastest.
Arguments:
- matrix_panel: bfloat16 [128, 1048576], P('col', 'row'), may hold values from -6 to 6
- row_signs: int32 [1048576], P('row'), may hold values from -1 to 1, as said below
- sample_rows: int32 [16384], replicated, may hold values from 0 to 1048575, as said below
Outputs:
- sketch: float32 [128, 16384], P('col', 'row')
- gram: float32 [128, 128], P('col')
Inputs may be any that keep to these rules, and one draw needn't show every extreme that they name: `row_signs`: each entry is -1 or +1. `sample_rows`: strictly increasing, so all distinct.
All inputs are finite; a program needn't handle non-finite values.
Results may differ from a plain program's by a relative error of at most 0.0003.
Values sent between devices are 32-bit elements; how exact they have to be, the bound alone decides.
A program may use at most 64 MiB of HBM per device.

v0:
```python
import jax
import jax.numpy as jnp
from jax import lax
from jax.sharding import PartitionSpec as P


def parity_sign(left, right, bit_count):
    common = jnp.bitwise_and(left, right)
    total = jnp.zeros_like(common)
    for bit_index in range(bit_count):
        total = total + jnp.bitwise_and(jnp.right_shift(common, bit_index), 1)
    return (1 - 2 * jnp.bitwise_and(total, 1)).astype(jnp.float32)


def hadamard(order_size):
    bit_count = order_size.bit_length() - 1
    row_index = jnp.arange(order_size, dtype=jnp.int32)
    return parity_sign(row_index[:, None], row_index[None, :], bit_count)


def local_mix(block, signs):
    columns, length = block.shape
    first_size = min(length, 256)
    second_size = length // first_size
    values = block.astype(jnp.float32) * signs.astype(jnp.float32)[None, :]
    values = values.reshape(columns, first_size, second_size)
    values = jnp.einsum(
        "cab,ad->cdb", values, hadamard(first_size), precision=lax.Precision.HIGHEST
    )
    values = jnp.einsum(
        "cdb,be->cde", values, hadamard(second_size), precision=lax.Precision.HIGHEST
    )
    return values.reshape(columns, length) / jnp.sqrt(jnp.float32(length))


def body(matrix_panel, row_signs, sample_rows):
    devices = lax.axis_size("row")
    position = lax.axis_index("row")
    bit_count = devices.bit_length() - 1
    columns, length = matrix_panel.shape
    everything = sample_rows.shape[0]
    mixed = local_mix(matrix_panel, row_signs)
    owner = sample_rows // length
    offset = sample_rows - owner * length
    chosen = jnp.take(mixed, offset, axis=1)
    weights = parity_sign(owner, position, bit_count)
    summed = lax.psum_scatter(chosen * weights[None, :], "row", scatter_dimension=1, tiled=True)
    sketch = summed / jnp.sqrt(jnp.float32(devices))
    gathered = lax.all_gather(sketch, "col", axis=0, tiled=True)
    partial_gram = jnp.dot(gathered, gathered.T, precision=lax.Precision.HIGHEST)
    totals = lax.psum(partial_gram, "row")
    own_rows = lax.dynamic_slice_in_dim(totals, lax.axis_index("col") * columns, columns, 0)
    gram = own_rows / everything
    return (sketch, gram)


def solution(mesh):
    return jax.shard_map(
        body,
        mesh=mesh,
        in_specs=(P("col", "row"), P("row"), P()),
        out_specs=(P("col", "row"), P("col", None)),
        check_vma=False,
    )
```

profile of v0, /device:TPU:16, one launch (start us, length us, event | category | flops | bytes accessed | tf_op | source)
XLA Modules:
  0.0 1611.6 jit_solution(2291911694017970471)
XLA Ops:
  7.2 0.0 reduce-scatter.2.cloned.1.call-start
  7.2 0.9 compare_and_fusion
  8.1 1.0 subtract_convert_fusion
  9.1 0.8 convert_element_type.17
  9.8 1.4 convert_multiply_fusion
  11.3 2.7 copy.9
  14.0 4.5 copy.10
  18.4 2.2 fusion
  20.6 1.9 convolution_multiply_fusion
  22.5 4.5 copy.11
  27.0 56.9 %gather_fusion = f32[16384,64]{1,0:T(8,128)} fusion(f32[64,8192]{0,1:T(8,128)} %bitcast.17, s32[16384]{0:T(1024)S(1)} %get-tuple-element.9), kind=kCustom, calls=%fused_computation | custom fusion | bytes 8454144 | tf_op jit(solution)/shard_map/jit(_take)/gather | solution.py:45
  83.9 7.6 multiply_bitcast_fusion
  91.5 0.0 reduce-scatter.2.cloned.1.call-update
  91.5 0.0 all-reduce.2.cloned.1.call-start
  91.6 578.9 %reduce-scatter.2.cloned.1.call-done = f32[64,128]{0,1:T(8,128)} async-done(((f32[64,16384]{0,1:T(8,128)}), f32[64,128]{0,1:T(8,128)}) %reduce-scatter.2.cloned.1.call-update) | async-done | bytes 32784 | tf_op jit(solution)/shard_map/reduce_scatter | solution.py:47
  670.5 0.8 broadcast_multiply_fusion
  671.3 0.1 copy.13
  671.4 0.0 copy-start
  671.4 6.1 all_gather.3
  677.5 0.9 fusion.81
  678.4 0.0 all-reduce.2.cloned.1.call-update
  678.4 925.0 %all-reduce.2.cloned.1.call-done = f32[128,128]{1,0:T(8,128)} async-done(((f32[128,128]{1,0:T(8,128)}), f32[128,128]{1,0:T(8,128)}) %all-reduce.2.cloned.1.call-update) | async-done | bytes 65552 | tf_op jit(solution)/shard_map/psum | solution.py:51
  1603.4 1.4 dynamic-slice_multiply_fusion
  1604.8 0.0 copy-done
Async XLA Ops:
  7.2 663.3 %reduce-scatter.2.cloned.1.call-start = ((), (), s32[]{:S(2)}) async-start(), calls=%async_computation.1 | async-start | bytes 8454144 | tf_op jit(solution)/shard_map/reduce_scatter | solution.py:47
  91.5 1511.9 %all-reduce.2.cloned.1.call-start = ((), (), s32[]{:S(2)}) async-start(), calls=%async_computation.2 | async-start | bytes 131072 | tf_op jit(solution)/shard_map/psum | solution.py:51
  671.4 933.4 %copy-start = (f32[64,128]{1,0:T(8,128)}, f32[64,128]{1,0:T(8,128)S(1)}, u32[]{:S(2)}) copy-start(f32[64,128]{1,0:T(8,128)S(1)} %copy.13) | copy-start | bytes 98308
Sparse Core Ops, SparseCore 0:
  91.6 578.7 reduce-scatter.1
  678.5 924.8 all-reduce.1
where the time goes:
time: 1610 us
  waiting for transfers between devices  1500 us (93%)
  local copies, waits for them, and re-layouts  68.7 us (4%)
    psum x1, waiting for transfers between devices, body(): totals = lax.psum(partial_gram, 'row')  925 us
    reduce_scatter x1, waiting for transfers between devices, body(): lax.psum_scatter(chosen * weights[None, :], 'row', scatter_dimension=1, t...  579 us
    gather x1, local copies, waits for them, and re-layouts, body(): chosen = jnp.take(mixed, offset, axis=1)  56.9 us
  transfers between devices with their start and end apart: 2, of which 2 were waited for; matrix products, arithmetic and copies ran while one was open for 0% of the time, Pallas kernels for 0%

commit v1 on v0

--- a/solution.py
+++ b/solution.py
@@ -48,7 +48,7 @@
     sketch = summed / jnp.sqrt(jnp.float32(devices))
     gathered = lax.all_gather(sketch, "col", axis=0, tiled=True)
     partial_gram = jnp.dot(gathered, gathered.T, precision=lax.Precision.HIGHEST)
-    totals = lax.psum(partial_gram, "row")
+    totals = jnp.sum(lax.all_gather(partial_gram, "row"), axis=0)
     own_rows = lax.dynamic_slice_in_dim(totals, lax.axis_index("col") * columns, columns, 0)
     gram = own_rows / everything
     return (sketch, gram)

time: 1610 us -> 908 us (0.56)
  waiting for transfers between devices: 1500 us -> 796 us
    psum x1 -> x0, waiting for transfers between devices: 925 us -> none  [body(): totals = lax.psum(partial_gram, 'row')]
    all_gather x0 -> x1, waiting for transfers between devices: none -> 217 us  [body(): totals = jnp.sum(lax.all_gather(partial_gram, 'row'), axis=0)]
where the time goes in v1:
time: 908 us; the launch traced here: 907 us
  waiting for transfers between devices  796 us (88%)
  local copies, waits for them, and re-layouts  68.7 us (8%)
  other arithmetic  16.9 us (2%)
  between operations  14.1 us (2%)
    reduce_scatter x1, waiting for transfers between devices, body(): lax.psum_scatter(chosen * weights[None, :], 'row', scatter_dimension=1, t...  579 us
    all_gather x1, waiting for transfers between devices, body(): totals = jnp.sum(lax.all_gather(partial_gram, 'row'), axis=0)  217 us
    gather x1, local copies, waits for them, and re-layouts, body(): chosen = jnp.take(mixed, offset, axis=1)  56.9 us
  transfers between devices with their start and end apart: 2, of which 2 were waited for; matrix products, arithmetic and copies ran while one was open for 0% of the time, Pallas kernels for 0%

profile of v1, /device:TPU:16, one launch (start us, length us, event | category | flops | bytes accessed | tf_op | source)
XLA Modules:
  0.0 906.7 jit_solution(9000969744784904402)
XLA Ops:
  7.2 0.0 reduce-scatter.2.cloned.1.call-start
  7.2 0.9 compare_and_fusion
  8.1 1.0 subtract_convert_fusion
  9.1 0.8 convert_element_type.17
  9.8 1.4 convert_multiply_fusion
  11.3 2.7 copy.9
  14.0 4.5 copy.10
  18.4 2.2 fusion
  20.6 1.9 convolution_multiply_fusion
  22.5 4.5 copy.11
  27.0 56.9 %gather_fusion = f32[16384,64]{1,0:T(8,128)} fusion(f32[64,8192]{0,1:T(8,128)} %bitcast.18, s32[16384]{0:T(1024)S(1)} %get-tuple-element.9), kind=kCustom, calls=%fused_computation | custom fusion | bytes 8454144 | tf_op jit(solution)/shard_map/jit(_take)/gather | solution.py:45
  83.9 7.6 multiply_bitcast_fusion
  91.5 0.0 reduce-scatter.2.cloned.1.call-update
  91.5 0.0 all-gather.3.cloned.1.call-start
  91.6 578.9 %reduce-scatter.2.cloned.1.call-done = f32[64,128]{0,1:T(8,128)} async-done(((f32[64,16384]{0,1:T(8,128)}), f32[64,128]{0,1:T(8,128)}) %reduce-scatter.2.cloned.1.call-update) | async-done | bytes 32784 | tf_op jit(solution)/shard_map/reduce_scatter | solution.py:47
  670.5 0.8 broadcast_multiply_fusion
  671.3 0.1 copy.13
  671.4 0.0 copy-start
  671.4 6.1 all_gather.9
  677.5 0.9 fusion.81
  678.4 0.0 all-gather.3.cloned.1.call-update
  678.4 217.0 %all-gather.3.cloned.1.call-done = f32[16384,128]{1,0:T(8,128)} async-done(((f32[128,128]{1,0:T(8,128)}), f32[16384,128]{1,0:T(8,128)}) %all-gather.3.cloned.1.call-update) | async-done | bytes 8388624 | tf_op jit(solution)/shard_map/all_gather | solution.py:51
  895.4 3.8 reduce_sum.9
  899.2 0.0 copy-done
  899.2 0.6 dynamic-slice_multiply_fusion
Async XLA Ops:
  7.2 663.3 %reduce-scatter.2.cloned.1.call-start = ((), (), s32[]{:S(2)}) async-start(), calls=%async_computation.1 | async-start | bytes 8454144 | tf_op jit(solution)/shard_map/reduce_scatter | solution.py:47
  91.5 803.9 %all-gather.3.cloned.1.call-start = ((), (), s32[]{:S(2)}) async-start(), calls=%async_computation.2 | async-start | bytes 8454144 | tf_op jit(solution)/shard_map/all_gather | solution.py:51
  671.4 227.8 %copy-start = (f32[64,128]{1,0:T(8,128)}, f32[64,128]{1,0:T(8,128)S(1)}, u32[]{:S(2)}) copy-start(f32[64,128]{1,0:T(8,128)S(1)} %copy.13) | copy-start | bytes 98308
Sparse Core Ops, SparseCore 0:
  91.6 578.7 reduce-scatter.1
  678.5 216.8 all-gather.2
